TPU v7x, 512 devices: a whole 4x8x8 slice. The times are simulated.
512 devices in a mesh: island: 16 (over y_hi, x), expert: 32 (over z, y_lo, core).
Axes of the slice: x: 4, y: 8 (y_hi: 4, y_lo: 2; y = y_hi * 2 + y_lo), z: 8, core: 2. Of those that a mesh axis runs over, the one named last changes fastest.
Arguments:
- tokens: bfloat16 [1, 65536, 5120], P(None, ('island', 'expert')), may hold values from -6 to 6
- targets: bfloat16 [1, 65536, 5120], P(None, ('island', 'expert')), may hold values from -6 to 6
- expert_ids: int32 [1, 65536, 6], P(None, ('island', 'expert')), may hold values from 0 to 159, as said below
- gate_weights: float32 [1, 65536, 6], P(None, ('island', 'expert')), may hold values from 0.1 to 1
- gate_proj: bfloat16 [3072, 5120], P('expert', 'island'), may hold values from -0.078125 to 0.078125
- up_proj: bfloat16 [3072, 5120], P('expert', 'island'), may hold values from -0.078125 to 0.078125
- down_global: float32 [3072, 5120], P('expert', 'island'), may hold values from -0.21875 to 0.21875
- outer_momentum: float32 [3072, 5120], P('expert', 'island'), may hold values from -0.003 to 0.003
- inner_first: bfloat16 [16, 3072, 5120], P('island', 'expert'), may hold values from -1.1953125 to 1.1953125
- inner_second: bfloat16 [16, 3072, 5120], P('island', 'expert'), may hold values from 0.5 to 8
Outputs:
- new_down: float32 [3072, 5120], P('expert', 'island')
- new_momentum: float32 [3072, 5120], P('expert', 'island')
Inputs may be any that keep to these rules, and one draw needn't show every extreme that they name: `expert_ids`: A row's 6 ids are different. In each inner step and each aligned block of 128 rows (the rows of one device), a row names at most one id below 4, each id below 4 is named by at most 8 rows, and in every block one of them is named by exactly 8 rows.
All inputs are finite; a program needn't handle non-finite values.
Results may differ from a plain program's by a relative error of at most 0.0051.
Values may be sent and summed in bfloat16 or wider, within the bound.
A program may use at most 64 MiB of HBM per device.

v0:
```python
import jax
import jax.numpy as jnp
from jax import lax
from jax.sharding import PartitionSpec as P

GROUP = 8
CAP = 8
beta_first = 0.9
beta_second = 0.95
inner_rate = 0.01
decay_rate = 0.1
epsilon = 1e-08
outer_rate = 0.7
outer_mu = 0.9


def route_table(expert_ids, gate_weights, window):
    hit = expert_ids < window
    chosen = jnp.sum(jnp.where(hit, expert_ids, 0), axis=1)
    routed = jnp.any(hit, axis=1)
    weight = jnp.sum(jnp.where(hit, gate_weights, jnp.zeros_like(gate_weights)), axis=1)
    member = (chosen[:, None] == jnp.arange(window, dtype=jnp.int32)[None, :]) & routed[:, None]
    rank = jnp.cumsum(member.astype(jnp.int32), axis=0) - 1
    places = member[:, :, None] & (
        rank[:, :, None] == jnp.arange(CAP, dtype=jnp.int32)[None, None, :]
    )
    select = places.reshape(expert_ids.shape[0], window * CAP).T.astype(jnp.float32)
    return (select, weight)


def outbound(select, values, window):
    picked = jnp.dot(select.astype(jnp.bfloat16), values, preferred_element_type=jnp.float32)
    return jnp.repeat(picked.astype(jnp.bfloat16).reshape(window, CAP, -1), GROUP, axis=0)


def on_device(
    tokens,
    targets,
    expert_ids,
    gate_weights,
    gate_proj,
    up_proj,
    down_global,
    outer_momentum,
    inner_first,
    inner_second,
):
    devices = lax.axis_size("expert")
    window = devices // GROUP
    islands = lax.axis_size("island")
    width = tokens.shape[2]
    weights = lax.all_gather(down_global, "island", axis=1, tiled=True)
    gate_full, up_full = (
        lax.all_gather(gate_proj, "island", axis=1, tiled=True),
        lax.all_gather(up_proj, "island", axis=1, tiled=True),
    )
    start_weights = weights
    first = inner_first[0].astype(jnp.float32)
    second = inner_second[0].astype(jnp.float32)
    select, weight = route_table(expert_ids[0], gate_weights[0], window)
    rows = lax.all_to_all(
        outbound(select, tokens[0], window), "expert", split_axis=0, concat_axis=0, tiled=True
    ).reshape(-1, width)
    pre_gate = jnp.einsum("rd,hd->rh", rows, gate_full, preferred_element_type=jnp.float32)
    pre_up = jnp.einsum("rd,hd->rh", rows, up_full, preferred_element_type=jnp.float32)
    active = (jax.nn.silu(pre_gate) * pre_up).astype(jnp.bfloat16)
    partial_value = jnp.dot(
        active, weights.astype(jnp.bfloat16), preferred_element_type=jnp.float32
    )
    partial_value = partial_value.reshape(devices, CAP, width)
    returned = lax.all_to_all(partial_value, "expert", split_axis=0, concat_axis=0, tiled=True)
    output = jnp.sum(returned.reshape(window, GROUP, CAP, width), axis=1)
    aims = jnp.dot(
        select.astype(jnp.bfloat16), targets[0], preferred_element_type=jnp.float32
    ).reshape(window, CAP, width)
    scales = jnp.dot(select, weight, precision=lax.Precision.HIGHEST).reshape(window, CAP, 1)
    errors = (scales * (scales * output - aims)).astype(jnp.bfloat16)
    landed = lax.all_to_all(
        jnp.repeat(errors, GROUP, axis=0), "expert", split_axis=0, concat_axis=0, tiled=True
    ).reshape(-1, width)
    grads = jnp.einsum("rh,rd->hd", active, landed, preferred_element_type=jnp.float32)
    first = beta_first * first + (1.0 - beta_first) * grads
    second = beta_second * second + (1.0 - beta_second) * grads * grads
    weights = weights - inner_rate * (first / (jnp.sqrt(second) + epsilon) + decay_rate * weights)
    delta = start_weights - weights
    columns = down_global.shape[1]
    total = lax.psum(delta, "island")
    mine = lax.dynamic_slice_in_dim(total, lax.axis_index("island") * columns, columns, 1)
    mean = mine / islands
    new_momentum = outer_mu * outer_momentum + mean
    new_down = down_global - outer_rate * (mean + outer_mu * new_momentum)
    return (new_down, new_momentum)


def solution(mesh):
    return jax.shard_map(
        on_device,
        mesh=mesh,
        in_specs=(
            P(None, ("island", "expert"), None),
            P(None, ("island", "expert"), None),
            P(None, ("island", "expert"), None),
            P(None, ("island", "expert"), None),
            P("expert", "island"),
            P("expert", "island"),
            P("expert", "island"),
            P("expert", "island"),
            P("island", "expert", None),
            P("island", "expert", None),
        ),
        out_specs=(P("expert", "island"), P("expert", "island")),
        check_vma=False,
    )
```

profile of v0, /device:TPU:64, one launch (start us, length us, event | category | flops | bytes accessed | tf_op | source)
XLA Modules:
  0.0 602.1 jit_solution(15182148449212197622)
XLA Ops:
  7.2 0.8 fusion.42
  8.0 0.7 fusion.44
  8.7 0.1 fusion.25
  8.8 0.2 reduce_window_sum.11
  9.0 0.1 copy.22
  9.0 0.1 copy.21
  9.1 0.1 eq.47
  9.2 0.4 fusion.2
  9.6 1.8 broadcast_in_dim.20
  11.4 11.3 %all-to-all-start = ((bf16[32,8,5120]{2,1,0:T(8,128)(2,1)}), bf16[32,8,5120]{2,1,0:T(8,128)(2,1)}, u32[]{:S(2)}, u32[]{:S(2)}) async-start(bf16[32,8,5120]{2,1,0:T(8,128)(2,1)} %bitcast.127), calls=%async_computation | async-start | bytes 5242880 | tf_op jit(solution)/shard_map/all_to_all | solution.py:61
  22.8 0.7 all-gather.5.cloned.1.call-update
  23.5 108.9 %all-gather.1 = bf16[16,320,96]{1,2,0:T(8,128)(2,1)S(1)} all-gather(bf16[1,320,96]{1,2,0:T(8,128)(2,1)S(1)} %bitcast.130), channel_id=1, replica_groups=mesh['island'=16,'expert'=32] {'island'}, dimensions={0}, use_global_device_ids=true | all-gather | bytes 1044480 | tf_op jit(solution)/shard_map/all_gather | solution.py:54
  132.4 0.4 copy.23
  132.8 1.7 reshape.129
  134.6 49.5 %all-gather.2 = bf16[16,320,96]{1,2,0:T(8,128)(2,1)S(1)} all-gather(bf16[1,320,96]{1,2,0:T(8,128)(2,1)S(1)} %bitcast.131), channel_id=1, replica_groups=mesh['island'=16,'expert'=32] {'island'}, dimensions={0}, use_global_device_ids=true | all-gather | bytes 1044480 | tf_op jit(solution)/shard_map/all_gather | solution.py:55
  184.1 0.4 copy.24
  184.5 1.8 reshape.131
  186.3 4.5 copy.20
  190.8 2.0 reshape.127
  192.8 3.0 fusion.7
  195.9 2.7 fusion.22
  198.6 3.2 convolution_bitcast_fusion
  201.8 13.4 %all-to-all-start.1 = ((f32[32,8,5120]{2,1,0:T(8,128)}), f32[32,8,5120]{2,1,0:T(8,128)}, u32[]{:S(2)}, u32[]{:S(2)}) async-start(f32[32,8,5120]{2,1,0:T(8,128)} %convolution_bitcast_fusion), calls=%async_computation.1 | async-start | bytes 10485760 | tf_op jit(solution)/shard_map/all_to_all | solution.py:71
  215.3 0.3 fusion.28
  215.6 116.1 %all-to-all-done.1 = f32[32,8,5120]{2,1,0:T(8,128)} async-done(((f32[32,8,5120]{2,1,0:T(8,128)}), f32[32,8,5120]{2,1,0:T(8,128)}, u32[]{:S(2)}, u32[]{:S(2)}) %all-to-all-start.1) | async-done | bytes 5242912 | tf_op jit(solution)/shard_map/all_to_all | solution.py:71
  331.6 2.9 bitcast_reduce_fusion
  334.6 0.4 fusion.1
  334.9 0.3 broadcast_in_dim.22
  335.2 79.1 %all_to_all.15 = bf16[32,8,5120]{2,1,0:T(8,128)(2,1)S(1)} all-to-all(bf16[32,8,5120]{2,1,0:T(8,128)(2,1)S(1)} %bitcast.128), channel_id=1, replica_groups=mesh['island'=16,'expert'=32] {'expert'}, dimensions={0} | all-to-all | bytes 5242880 | tf_op jit(solution)/shard_map/all_to_all | solution.py:78
  414.3 3.2 subtract_subtract_fusion
  417.5 176.0 %all-reduce.2.cloned.1.call-done = f32[96,5120]{1,0:T(8,128)} async-done(((f32[96,5120]{1,0:T(8,128)}), f32[96,5120]{1,0:T(8,128)}) %all-reduce.2.cloned.1.call-update) | async-done | bytes 1966096 | tf_op jit(solution)/shard_map/psum | solution.py:87
  593.5 1.7 multiply_subtract_fusion
  (30 shorter events, 0.2 us)
Async XLA Ops:
  7.2 2.1 copy-start
  11.4 12.1 %copy-start.5 = (bf16[96,320]{1,0:T(8,128)(2,1)S(1)}, bf16[96,320]{1,0:T(8,128)(2,1)}, u32[]{:S(2)}) copy-start(bf16[96,320]{1,0:T(8,128)(2,1)} %param.14) | copy-start | bytes 184324
  11.4 181.4 %all-to-all-start = ((bf16[32,8,5120]{2,1,0:T(8,128)(2,1)}), bf16[32,8,5120]{2,1,0:T(8,128)(2,1)}, u32[]{:S(2)}, u32[]{:S(2)}) async-start(bf16[32,8,5120]{2,1,0:T(8,128)(2,1)} %bitcast.127), calls=%async_computation | async-start | bytes 5242880 | tf_op jit(solution)/shard_map/all_to_all | solution.py:61
  22.7 163.5 %all-gather.5.cloned.1.call-start = ((), (), s32[]{:S(2)}) async-start(), calls=%async_computation.4 | async-start | bytes 2506752 | tf_op jit(solution)/shard_map/all_gather | solution.py:52
  132.4 2.1 copy-start.6
  192.8 3.0 copy-start.1
  201.8 13.5 %copy-start.7 = (s32[1,128,6]{1,0,2:T(1,128)S(1)}, s32[1,128,6]{1,0,2:T(1,128)}, u32[]{:S(2)}) copy-start(s32[1,128,6]{1,0,2:T(1,128)} %param.12) | copy-start | bytes 9220
  201.8 13.5 %copy-start.8 = (f32[1,128,6]{1,0,2:T(1,128)S(1)}, f32[1,128,6]{1,0,2:T(1,128)}, u32[]{:S(2)}) copy-start(f32[1,128,6]{1,0,2:T(1,128)} %param.13) | copy-start | bytes 9220
  201.8 129.9 %all-to-all-start.1 = ((f32[32,8,5120]{2,1,0:T(8,128)}), f32[32,8,5120]{2,1,0:T(8,128)}, u32[]{:S(2)}, u32[]{:S(2)}) async-start(f32[32,8,5120]{2,1,0:T(8,128)} %convolution_bitcast_fusion), calls=%async_computation.1 | async-start | bytes 10485760 | tf_op jit(solution)/shard_map/all_to_all | solution.py:71
  215.2 378.3 %all-reduce.2.cloned.1.call-start = ((), (), s32[]{:S(2)}) async-start(), calls=%async_computation.3 | async-start | bytes 3932160 | tf_op jit(solution)/shard_map/psum | solution.py:87
  331.6 2.9 copy-start.2
  335.2 79.1 %copy-start.9 = (bf16[1,96,5120]{2,1,0:T(8,128)(2,1)S(1)}, bf16[1,96,5120]{2,1,0:T(8,128)(2,1)}, u32[]{:S(2)}) copy-start(bf16[1,96,5120]{2,1,0:T(8,128)(2,1)} %param.19) | copy-start | bytes 2949124
  335.2 79.1 %copy-start.10 = (bf16[1,96,5120]{2,1,0:T(8,128)(2,1)S(1)}, bf16[1,96,5120]{2,1,0:T(8,128)(2,1)}, u32[]{:S(2)}) copy-start(bf16[1,96,5120]{2,1,0:T(8,128)(2,1)} %param.18) | copy-start | bytes 2949124
  417.5 176.1 %copy-start.3 = (f32[96,320]{1,0:T(8,128)S(1)}, f32[96,320]{1,0:T(8,128)}, u32[]{:S(2)}) copy-start(f32[96,320]{1,0:T(8,128)} %param.16) | copy-start | bytes 368644
  417.5 176.1 %copy-start.4 = (f32[96,320]{1,0:T(8,128)S(1)}, f32[96,320]{1,0:T(8,128)}, u32[]{:S(2)}) copy-start(f32[96,320]{1,0:T(8,128)} %param.17) | copy-start | bytes 368644
Sparse Core Ops, SparseCore 0:
  26.6 77.0 all-gather.4
  417.6 175.8 all-reduce.1
where the time goes:
time: 603 us; the launch traced here: 602 us
  waiting for transfers between devices  293 us (49%)
  blocking collectives  238 us (39%)
  starting transfers between devices  24.8 us (4%)
  between operations  14.2 us (2%)
  local copies, waits for them, and re-layouts  13.2 us (2%)
  matrix products  13.1 us (2%)
  other arithmetic  6.46 us (1%)
    psum x1, waiting for transfers between devices, on_device(): total = lax.psum(delta, 'island')  176 us
    all_to_all x1, waiting for transfers between devices, on_device(): lax.all_to_all(partial_value, 'expert', split_axis=0, concat_axis=0, tile...  116 us
    all_gather x1, blocking collectives, on_device(): lax.all_gather(gate_proj, 'island', axis=1, tiled=True)  109 us
    all_to_all x1, blocking collectives, on_device(): lax.all_to_all(jnp.repeat(errors, GROUP, axis=0), 'expert', split_axis=0,...  79.1 us
    all_gather x1, blocking collectives, on_device(): lax.all_gather(up_proj, 'island', axis=1, tiled=True)  49.5 us
    all_to_all x1, starting transfers between devices, on_device(): lax.all_to_all(partial_value, 'expert', split_axis=0, concat_axis=0, tile...  13.4 us
  transfers between devices with their start and end apart: 4, of which 2 were waited for; matrix products, arithmetic and copies ran while one was open for 2% of the time, Pallas kernels for 0%

commit v1 on v0

--- a/solution.py
+++ b/solution.py
@@ -84,7 +84,7 @@
     weights = weights - inner_rate * (first / (jnp.sqrt(second) + epsilon) + decay_rate * weights)
     delta = start_weights - weights
     columns = down_global.shape[1]
-    total = lax.psum(delta, "island")
+    total = jnp.sum(lax.all_gather(delta, "island"), axis=0)
     mine = lax.dynamic_slice_in_dim(total, lax.axis_index("island") * columns, columns, 1)
     mean = mine / islands
     new_momentum = outer_mu * outer_momentum + mean

time: 603 us -> 792 us (1.31)
  the two profiles are of different devices: /device:TPU:64 before, /device:TPU:1 now
where the time goes in v1:
time: 792 us
  waiting for transfers between devices  475 us (60%)
  blocking collectives  211 us (27%)
  starting transfers between devices  47.8 us (6%)
  other arithmetic  17.9 us (2%)
  between operations  14.2 us (2%)
  local copies, waits for them, and re-layouts  13.3 us (2%)
  matrix products  12.9 us (2%)
    all_gather x1, waiting for transfers between devices, on_device(): total = jnp.sum(lax.all_gather(delta, 'island'), axis=0)  352 us
    all_to_all x1, waiting for transfers between devices, on_device(): lax.all_to_all(partial_value, 'expert', split_axis=0, concat_axis=0, tile...  122 us
    all_gather x1, blocking collectives, on_device(): lax.all_gather(gate_proj, 'island', axis=1, tiled=True)  97.4 us
    all_to_all x1, blocking collectives, on_device(): lax.all_to_all(jnp.repeat(errors, GROUP, axis=0), 'expert', split_axis=0,...  74.1 us
    all_gather x1, blocking collectives, on_device(): lax.all_gather(up_proj, 'island', axis=1, tiled=True)  39.6 us
    all_to_all x1, starting transfers between devices, on_device(): lax.all_to_all(partial_value, 'expert', split_axis=0, concat_axis=0, tile...  34.6 us
  transfers between devices with their start and end apart: 4, of which 2 were waited for; matrix products, arithmetic and copies ran while one was open for 1% of the time, Pallas kernels for 0%

profile of v1, /device:TPU:1, one launch (start us, length us, event | category | flops | bytes accessed | tf_op | source)
XLA Modules:
  0.0 791.8 jit_solution(1827772880916002212)
XLA Ops:
  7.2 0.8 fusion.42
  8.0 0.7 fusion.44
  8.7 0.1 fusion.25
  8.8 0.2 reduce_window_sum.11
  9.0 0.1 copy.21
  9.1 0.1 eq.47
  9.2 0.4 fusion.2
  9.6 1.8 broadcast_in_dim.20
  11.4 13.2 %all-to-all-start = ((bf16[32,8,5120]{2,1,0:T(8,128)(2,1)}), bf16[32,8,5120]{2,1,0:T(8,128)(2,1)}, u32[]{:S(2)}, u32[]{:S(2)}) async-start(bf16[32,8,5120]{2,1,0:T(8,128)(2,1)} %bitcast.129), calls=%async_computation | async-start | bytes 5242880 | tf_op jit(solution)/shard_map/all_to_all | solution.py:61
  24.6 0.7 all-gather.9.cloned.1.call-update
  25.3 97.4 %all-gather.2 = bf16[16,320,96]{1,2,0:T(8,128)(2,1)S(1)} all-gather(bf16[1,320,96]{1,2,0:T(8,128)(2,1)S(1)} %bitcast.132), channel_id=1, replica_groups=mesh['island'=16,'expert'=32] {'island'}, dimensions={0}, use_global_device_ids=true | all-gather | bytes 1044480 | tf_op jit(solution)/shard_map/all_gather | solution.py:54
  122.7 0.4 copy.23
  123.1 1.7 reshape.130
  124.9 39.6 %all-gather.3 = bf16[16,320,96]{1,2,0:T(8,128)(2,1)S(1)} all-gather(bf16[1,320,96]{1,2,0:T(8,128)(2,1)S(1)} %bitcast.133), channel_id=1, replica_groups=mesh['island'=16,'expert'=32] {'island'}, dimensions={0}, use_global_device_ids=true | all-gather | bytes 1044480 | tf_op jit(solution)/shard_map/all_gather | solution.py:55
  164.5 0.4 copy.24
  164.9 1.8 reshape.132
  166.7 4.5 copy.20
  171.2 2.1 reshape.128
  173.3 2.8 fusion.7
  176.1 2.7 fusion.22
  178.8 3.2 convolution_bitcast_fusion
  182.0 34.6 %all-to-all-start.1 = ((f32[32,8,5120]{2,1,0:T(8,128)}), f32[32,8,5120]{2,1,0:T(8,128)}, u32[]{:S(2)}, u32[]{:S(2)}) async-start(f32[32,8,5120]{2,1,0:T(8,128)} %convolution_bitcast_fusion), calls=%async_computation.1 | async-start | bytes 10485760 | tf_op jit(solution)/shard_map/all_to_all | solution.py:71
  216.7 0.3 fusion.28
  216.9 122.3 %all-to-all-done.1 = f32[32,8,5120]{2,1,0:T(8,128)} async-done(((f32[32,8,5120]{2,1,0:T(8,128)}), f32[32,8,5120]{2,1,0:T(8,128)}, u32[]{:S(2)}, u32[]{:S(2)}) %all-to-all-start.1) | async-done | bytes 5242912 | tf_op jit(solution)/shard_map/all_to_all | solution.py:71
  339.3 2.9 bitcast_reduce_fusion
  342.2 0.4 fusion.1
  342.6 0.3 broadcast_in_dim.22
  342.9 74.1 %all_to_all.15 = bf16[32,8,5120]{2,1,0:T(8,128)(2,1)S(1)} all-to-all(bf16[32,8,5120]{2,1,0:T(8,128)(2,1)S(1)} %bitcast.130), channel_id=1, replica_groups=mesh['island'=16,'expert'=32] {'expert'}, dimensions={0} | all-to-all | bytes 5242880 | tf_op jit(solution)/shard_map/all_to_all | solution.py:78
  417.0 3.2 subtract_subtract_fusion
  420.2 351.6 %all-gather.7.cloned.1.call-done = f32[1536,5120]{1,0:T(8,128)} async-done(((f32[96,5120]{1,0:T(8,128)}), f32[1536,5120]{1,0:T(8,128)}) %all-gather.7.cloned.1.call-update) | async-done | bytes 31457296 | tf_op jit(solution)/shard_map/all_gather | solution.py:87
  771.8 11.4 %reduce_sum.39 = f32[96,5120]{1,0:T(8,128)S(1)} reduce(f32[16,96,5120]{2,1,0:T(8,128)} %bitcast.128, f32[]{:T(128)} %constant.10.clone.1), dimensions={0}, to_apply=%region_5.6 | reduce | flops 7372800 | bytes 33423364 | tf_op jit(solution)/shard_map/reduce_sum | solution.py:87
  783.2 1.7 multiply_subtract_fusion
  (33 shorter events, 0.3 us)
Async XLA Ops:
  7.2 2.1 copy-start
  11.4 13.9 %copy-start.6 = (bf16[96,320]{1,0:T(8,128)(2,1)S(1)}, bf16[96,320]{1,0:T(8,128)(2,1)}, u32[]{:S(2)}) copy-start(bf16[96,320]{1,0:T(8,128)(2,1)} %param.14) | copy-start | bytes 184324
  11.4 161.9 %all-to-all-start = ((bf16[32,8,5120]{2,1,0:T(8,128)(2,1)}), bf16[32,8,5120]{2,1,0:T(8,128)(2,1)}, u32[]{:S(2)}, u32[]{:S(2)}) async-start(bf16[32,8,5120]{2,1,0:T(8,128)(2,1)} %bitcast.129), calls=%async_computation | async-start | bytes 5242880 | tf_op jit(solution)/shard_map/all_to_all | solution.py:61
  24.6 142.1 %all-gather.9.cloned.1.call-start = ((), (), s32[]{:S(2)}) async-start(), calls=%async_computation.4 | async-start | bytes 2506752 | tf_op jit(solution)/shard_map/all_gather | solution.py:52
  122.7 2.1 copy-start.7
  171.2 2.1 copy-start.2
  173.3 2.8 copy-start.3
  182.0 34.6 %copy-start.8 = (s32[1,128,6]{1,0,2:T(1,128)S(1)}, s32[1,128,6]{1,0,2:T(1,128)}, u32[]{:S(2)}) copy-start(s32[1,128,6]{1,0,2:T(1,128)} %param.12) | copy-start | bytes 9220
  182.0 34.6 %copy-start.9 = (f32[1,128,6]{1,0,2:T(1,128)S(1)}, f32[1,128,6]{1,0,2:T(1,128)}, u32[]{:S(2)}) copy-start(f32[1,128,6]{1,0,2:T(1,128)} %param.13) | copy-start | bytes 9220
  182.0 157.3 %all-to-all-start.1 = ((f32[32,8,5120]{2,1,0:T(8,128)}), f32[32,8,5120]{2,1,0:T(8,128)}, u32[]{:S(2)}, u32[]{:S(2)}) async-start(f32[32,8,5120]{2,1,0:T(8,128)} %convolution_bitcast_fusion), calls=%async_computation.1 | async-start | bytes 10485760 | tf_op jit(solution)/shard_map/all_to_all | solution.py:71
  216.6 555.2 %all-gather.7.cloned.1.call-start = ((), (), s32[]{:S(2)}) async-start(), calls=%async_computation.3 | async-start | bytes 33423360 | tf_op jit(solution)/shard_map/all_gather | solution.py:87
  339.3 2.9 copy-start.4
  342.9 74.1 %copy-start.10 = (bf16[1,96,5120]{2,1,0:T(8,128)(2,1)S(1)}, bf16[1,96,5120]{2,1,0:T(8,128)(2,1)}, u32[]{:S(2)}) copy-start(bf16[1,96,5120]{2,1,0:T(8,128)(2,1)} %param.19) | copy-start | bytes 2949124
  342.9 74.1 %copy-start.11 = (bf16[1,96,5120]{2,1,0:T(8,128)(2,1)S(1)}, bf16[1,96,5120]{2,1,0:T(8,128)(2,1)}, u32[]{:S(2)}) copy-start(bf16[1,96,5120]{2,1,0:T(8,128)(2,1)} %param.18) | copy-start | bytes 2949124
  771.8 11.4 %copy-start.5 = (f32[96,320]{1,0:T(8,128)S(1)}, f32[96,320]{1,0:T(8,128)}, u32[]{:S(2)}) copy-start(f32[96,320]{1,0:T(8,128)} %param.16) | copy-start | bytes 368644
  771.8 13.2 %copy-start.1 = (bf16[1,128,5120]{2,1,0:T(8,128)(2,1)S(1)}, bf16[1,128,5120]{2,1,0:T(8,128)(2,1)}, u32[]{:S(2)}) copy-start(bf16[1,128,5120]{2,1,0:T(8,128)(2,1)} %param.10) | copy-start | bytes 3932164
Sparse Core Ops, SparseCore 0:
  28.4 73.7 all-gather.8
  420.3 351.4 all-gather.6
